TPU v7x, 32 devices: a whole 2x2x4 slice. The times are simulated.
32 devices in a mesh: groups: 2 (over y), feat: 8 (over z, x), corp: 2 (over core).
Axes of the slice: x: 2, y: 2, z: 4, core: 2. Of those that a mesh axis runs over, the one named last changes fastest.
Arguments:
- query_features: bfloat16 [1536, 16384], P(('groups', 'corp'), 'feat'), parts along dimension 0, may hold values from -6 to 6
- inverse_kernel: bfloat16 [16384, 16384], P(None, 'feat'), may hold values from -1 to 3, as said below
- doc_features: bfloat16 [512, 16384], P(('groups', 'corp'), 'feat'), parts along dimension 0, may hold values from -0.046875 to 0.046875
Outputs:
- scores: float32 [1536, 256], P(('groups', 'feat'), 'corp'), parts along dimension 0
There are 2 independent parts, one for each index of `groups`. A program takes and returns all parts, laid end to end along the dimension named above; an argument that names none is the same for every part. Nothing has to cross between parts.
Inputs may be any that keep to these rules, and one draw needn't show every extreme that they name: inverse_kernel is symmetric.
All inputs are finite; a program needn't handle non-finite values.
Results may differ from a plain program's by a relative error of at most 0.0003.
Values may be sent and summed in bfloat16 or wider, within the bound.
A program may use at most 128 MiB of HBM per device.

v0:
```python
import functools

import jax
import jax.numpy as jnp
from jax import lax
from jax.experimental import pallas as pl
from jax.experimental.pallas import tpu as pltpu
from jax.sharding import PartitionSpec as P

MESH = pl.DeviceIdType.MESH
PIECES = 2
SLOTS = 8
TILE = 512


def plan(depth, pieces):
    keep = pieces // 2

    def partner(z):
        return z ^ 1 if depth % 2 == 0 else -1

    plans = []
    for z in range(depth):
        same = []
        for b in range(depth):
            for h in range(pieces):
                near = abs(b - z)
                when = 0 if near == 0 else pieces * (near - 1) + h + 1
                up = b <= z and z + 1 < depth
                down = b >= z and z > 0
                across = not (b == partner(z) and h >= keep)
                same.append((when, 1, b, h, up, down, across))
        same.sort(key=lambda e: (e[0], e[2] != partner(z), e[3]))
        other, clock = [], 0
        for when, _, b, h, _, _, across in same:
            if across:
                clock = max(clock, when) + 1
                sent = b == z and h >= keep and partner(z) >= 0
                up = sent and partner(z) > z
                down = sent and partner(z) < z
                other.append((clock + 0.5, 0, b, h, up, down, False))
        count = 0
        for b in range(depth):
            for h in range(keep, pieces):
                if b == partner(z):
                    count += 1
                    line = z + 1 if b < z else depth - z
                    if b > z:
                        line = depth - 1 - z
                    else:
                        line = z
                    other.append((pieces * line + count, 0, b, h, False, False, False))
        mine = [e for e in same if e[2] == z]
        rest = sorted([e for e in same if e[2] != z] + other, key=lambda e: e[0])
        plans.append([e[1:] for e in mine + rest])
    return plans


def kernel(
    feats, q_ref, k_ref, d_ref, out_ref,
    docs, queries, slabs, acc, split, part, got,
    slab_sem, own_sem, send_sem, recv_sem, q_sem, part_send, part_recv,
):
    depth = feats // 2
    f, c = lax.axis_index("feat"), lax.axis_index("corp")
    z, x = f // 2, f % 2
    plans = plan(depth, PIECES)
    steps = feats * PIECES
    width = docs.shape[2]
    n_docs = docs.shape[1]

    def pick(values):
        values = [int(v) for v in values]
        if len(set(values)) == 1:
            return values[0]
        result = jnp.int32(values[0])
        for at in range(1, depth):
            result = jnp.where(z == at, jnp.int32(values[at]), result)
        return result

    def event(n):
        same, b, h, up, down, across = (
            pick([plans[at][n][i] for at in range(depth)]) for i in range(6)
        )
        column = same * x + (1 - same) * (1 - x)
        return (b * 2 + column) * PIECES + h, up, down, across

    events = [event(n) for n in range(steps)]

    def slab_copy(n):
        p = events[n][0]
        return pltpu.make_async_copy(
            k_ref.at[pl.ds(pl.multiple_of(p * width, width), width), :],
            slabs.at[n % SLOTS],
            slab_sem.at[n % SLOTS],
        )

    own = [
        pltpu.make_async_copy(
            d_ref.at[:, pl.ds(h * width, width)], docs.at[f * PIECES + h], own_sem.at[h]
        )
        for h in range(PIECES)
    ]
    for copy in own:
        copy.start()
    own_q = pltpu.make_async_copy(q_ref, queries.at[c], q_sem.at[0])

    barrier = pltpu.get_barrier_semaphore()
    for away in range(1, feats):
        pl.semaphore_signal(
            barrier, inc=1, device_id={"feat": (f + away) % feats}, device_id_type=MESH
        )
    pl.semaphore_signal(barrier, inc=1, device_id={"corp": 1 - c}, device_id_type=MESH)
    for n in range(min(2, steps)):
        slab_copy(n).start()
    pl.semaphore_wait(barrier, feats)

    def piece_copy(p, way):
        to = (f + 2, f - 2, z * 2 + 1 - x)[way]
        return pltpu.make_async_remote_copy(
            src_ref=docs.at[p],
            dst_ref=docs.at[p],
            send_sem=send_sem.at[way, p],
            recv_sem=recv_sem.at[p],
            device_id={"feat": to},
            device_id_type=MESH,
        )

    def when(flag, action):
        if isinstance(flag, int):
            if flag:
                action()
        else:
            pl.when(flag == 1)(action)

    def pass_on(n):
        p, *ways = events[n]
        for way in (2, 0, 1):
            when(ways[way], lambda way=way: piece_copy(p, way).start())

    for n in range(PIECES):
        own[n].wait()
        pass_on(n)
    send_q = pltpu.make_async_remote_copy(
        src_ref=q_ref,
        dst_ref=queries.at[c],
        send_sem=q_sem.at[1],
        recv_sem=q_sem.at[2],
        device_id={"corp": 1 - c},
        device_id_type=MESH,
    )
    for n in range(min(2, steps), min(SLOTS, steps)):
        slab_copy(n).start()
    own_q.start()
    send_q.start()

    for n in range(steps):
        p = events[n][0]
        if n >= PIECES:
            piece_copy(p, 2).wait_recv()
            pass_on(n)
        slab_copy(n).wait()

        def tile(j, carry, n=n, p=p):
            columns = pl.ds(pl.multiple_of(j * TILE, TILE), TILE)
            term = jnp.dot(
                docs[p], slabs[n % SLOTS, :, columns], preferred_element_type=jnp.float32
            )
            acc[:, columns] = term if n == 0 else acc[:, columns] + term
            return carry

        lax.fori_loop(0, acc.shape[1] // TILE, tile, 0)
        if n + SLOTS < steps:
            slab_copy(n + SLOTS).start()

    high = acc[...].astype(jnp.bfloat16)
    split[:n_docs, :] = high
    split[n_docs:, :] = (acc[...] - high.astype(jnp.float32)).astype(jnp.bfloat16)
    own_q.wait()
    send_q.wait()

    rows = got.shape[1]
    halves = queries.shape[1] // rows

    def part_copy(to):
        return pltpu.make_async_remote_copy(
            src_ref=part.at[to],
            dst_ref=got.at[f],
            send_sem=part_send.at[to],
            recv_sem=part_recv.at[f],
            device_id={"feat": to},
            device_id_type=MESH,
        )

    def score(to):
        left = queries[to // halves, pl.ds(pl.multiple_of((to % halves) * rows, rows), rows), :]
        both = lax.dot_general(
            left, split[...], (((1,), (1,)), ((), ())), preferred_element_type=jnp.float32
        )
        return both[:, :n_docs] + both[:, n_docs:]

    def send_part(i, carry):
        to = (f + i) % feats
        part[to] = score(to)
        part_copy(to).start()
        return carry

    lax.fori_loop(1, feats, send_part, 0)
    got[f] = score(f)

    def take(i, carry):
        source = (f + i) % feats
        pltpu.make_async_remote_copy(
            src_ref=part.at[source],
            dst_ref=got.at[source],
            send_sem=part_send.at[source],
            recv_sem=part_recv.at[source],
            device_id={"feat": source},
            device_id_type=MESH,
        ).wait()
        return carry

    lax.fori_loop(1, feats, take, 0)
    total = got[0]
    for i in range(1, feats):
        total = total + got[i]
    out_ref[...] = total

    for n in range(steps):
        p, *ways = events[n]
        for way in range(3):
            when(ways[way], lambda way=way, p=p: piece_copy(p, way).wait_send())


def fused(feats, query_features, inverse_kernel, doc_features):
    n_docs, block = doc_features.shape
    n_queries = query_features.shape[0]
    rows = 2 * n_queries // feats
    width = block // PIECES
    return pl.pallas_call(
        functools.partial(kernel, feats),
        out_shape=jax.ShapeDtypeStruct((rows, n_docs), jnp.float32),
        in_specs=[pl.BlockSpec(memory_space=pl.ANY)] * 3,
        out_specs=pl.BlockSpec(memory_space=pltpu.VMEM),
        scratch_shapes=[
            pltpu.VMEM((feats * PIECES, n_docs, width), jnp.bfloat16),
            pltpu.VMEM((2, n_queries, block), jnp.bfloat16),
            pltpu.VMEM((SLOTS, width, block), jnp.bfloat16),
            pltpu.VMEM((n_docs, block), jnp.float32),
            pltpu.VMEM((2 * n_docs, block), jnp.bfloat16),
            pltpu.VMEM((feats, rows, n_docs), jnp.float32),
            pltpu.VMEM((feats, rows, n_docs), jnp.float32),
            pltpu.SemaphoreType.DMA((SLOTS,)),
            pltpu.SemaphoreType.DMA((PIECES,)),
            pltpu.SemaphoreType.DMA((3, feats * PIECES)),
            pltpu.SemaphoreType.DMA((feats * PIECES,)),
            pltpu.SemaphoreType.DMA((3,)),
            pltpu.SemaphoreType.DMA((feats,)),
            pltpu.SemaphoreType.DMA((feats,)),
        ],
        compiler_params=pltpu.CompilerParams(
            collective_id=0, has_side_effects=True, vmem_limit_bytes=56 * 2**20
        ),
        cost_estimate=pl.CostEstimate(
            flops=2 * n_docs * inverse_kernel.shape[0] * block,
            bytes_accessed=2 * inverse_kernel.shape[0] * block,
            transcendentals=0,
        ),
    )(query_features, inverse_kernel, doc_features)


def with_collectives(query_features, inverse_kernel, doc_features):
    applied = jnp.dot(
        lax.all_gather(doc_features, "feat", axis=1, tiled=True),
        inverse_kernel,
        preferred_element_type=jnp.float32,
    )
    left_rows = lax.all_gather(query_features, "corp", axis=0, tiled=True).astype(jnp.float32)
    return lax.psum_scatter(
        lax.dot_general(
            left_rows,
            applied,
            (((1,), (1,)), ((), ())),
            precision=lax.Precision.HIGHEST,
            preferred_element_type=jnp.float32,
        ),
        "feat",
        scatter_dimension=0,
        tiled=True,
    )


def solution(mesh):
    feats = mesh.shape["feat"]

    def on_device(query_features, inverse_kernel, doc_features):
        block, rows = doc_features.shape[1], 2 * query_features.shape[0] // feats
        fits = feats in (4, 8) and mesh.shape["corp"] == 2 and block % TILE == 0 and rows % 16 == 0
        if not fits:
            return with_collectives(query_features, inverse_kernel, doc_features)
        return fused(feats, query_features, inverse_kernel, doc_features)

    placed = (P(("groups", "corp"), "feat"), P(None, "feat"), P(("groups", "corp"), "feat"))
    return jax.shard_map(
        on_device,
        mesh=mesh,
        in_specs=placed,
        out_specs=P(("groups", "feat"), "corp"),
        check_vma=False,
    )
```

profile of v0, /device:TPU:0, one launch (start us, length us, event | category | flops | bytes accessed | tf_op | source)
XLA Modules:
  0.0 65.6 jit_solution(4635371865005688542)
XLA Ops:
  0.0 64.1 %shard_map.37 = f32[96,128]{1,0:T(8,128)} custom-call(bf16[384,2048]{1,0:T(8,128)(2,1)} %q_ref.1, bf16[16384,2048]{1,0:T(8,128)(2,1)} %k_ref.1, bf16[128,2048]{1,0:T(8,128)(2,1)} %d_ref.1), custom_call_target="tpu_custom_call" | custom-call | flops 8589934592 | bytes 67108864 | tf_op jit(solution)/shard_map/pallas_call | solution.py:240
  64.1 1.4 %copy.5 = f32[96,128]{1,0:T(8,128)} copy(f32[96,128]{1,0:T(8,128)} %shard_map.37) | data formatting | bytes 98304
where the time goes:
time: 65.7 us; the launch traced here: 65.6 us
  Pallas kernels  64.1 us (98%)
  local copies, waits for them, and re-layouts  1.42 us (2%)
    pallas_call x1, Pallas kernels, fused(): pl.pallas_call(functools.partial(kernel, feats), out_shape=jax.ShapeDtype...  64.1 us
    unnamed x1, local copies, waits for them, and re-layouts  1.42 us

commit v1 on v0

--- a/solution.py
+++ b/solution.py
@@ -8,8 +8,8 @@
 from jax.sharding import PartitionSpec as P
 
 MESH = pl.DeviceIdType.MESH
-PIECES = 2
-SLOTS = 8
+PIECES = 4
+SLOTS = 16
 TILE = 512
 
 
@@ -35,21 +35,13 @@
         for when, _, b, h, _, _, across in same:
             if across:
                 clock = max(clock, when) + 1
-                sent = b == z and h >= keep and partner(z) >= 0
-                up = sent and partner(z) > z
-                down = sent and partner(z) < z
-                other.append((clock + 0.5, 0, b, h, up, down, False))
+                other.append((clock + 0.5, 0, b, h, False, False, False))
         count = 0
         for b in range(depth):
             for h in range(keep, pieces):
                 if b == partner(z):
                     count += 1
-                    line = z + 1 if b < z else depth - z
-                    if b > z:
-                        line = depth - 1 - z
-                    else:
-                        line = z
-                    other.append((pieces * line + count, 0, b, h, False, False, False))
+                    other.append((2 * pieces * depth + count, 0, b, h, False, False, False))
         mine = [e for e in same if e[2] == z]
         rest = sorted([e for e in same if e[2] != z] + other, key=lambda e: e[0])
         plans.append([e[1:] for e in mine + rest])
@@ -65,6 +57,11 @@
     f, c = lax.axis_index("feat"), lax.axis_index("corp")
     z, x = f // 2, f % 2
     plans = plan(depth, PIECES)
+    detour = range(PIECES // 2, PIECES) if depth % 2 == 0 else range(0)
+    ready = [
+        max(n for n, e in enumerate(p) if e[0] == 1 or (e[1] == at and e[2] in detour))
+        for at, p in enumerate(plans)
+    ]
     steps = feats * PIECES
     width = docs.shape[2]
     n_docs = docs.shape[1]
@@ -116,7 +113,7 @@
     pl.semaphore_wait(barrier, feats)
 
     def piece_copy(p, way):
-        to = (f + 2, f - 2, z * 2 + 1 - x)[way]
+        to = (f + 2, f - 2, z * 2 + 1 - x, f + 2 - 4 * (z % 2))[way]
         return pltpu.make_async_remote_copy(
             src_ref=docs.at[p],
             dst_ref=docs.at[p],
@@ -133,10 +130,18 @@
         else:
             pl.when(flag == 1)(action)
 
+    def detours():
+        return [piece_copy((z * 2 + 1 - x) * PIECES + h, 3) for h in detour]
+
+    def start_detours():
+        for copy in detours():
+            copy.start()
+
     def pass_on(n):
         p, *ways = events[n]
         for way in (2, 0, 1):
             when(ways[way], lambda way=way: piece_copy(p, way).start())
+        when(pick([at == n for at in ready]), start_detours)
 
     for n in range(PIECES):
         own[n].wait()
@@ -180,7 +185,7 @@
     send_q.wait()
 
     rows = got.shape[1]
-    halves = queries.shape[1] // rows
+    halves = queries.shape[1] // (2 * rows)
 
     def part_copy(to):
         return pltpu.make_async_remote_copy(
@@ -192,21 +197,29 @@
             device_id_type=MESH,
         )
 
-    def score(to):
-        left = queries[to // halves, pl.ds(pl.multiple_of((to % halves) * rows, rows), rows), :]
+    def score(level):
+        start = pl.multiple_of((level % halves) * 2 * rows, 2 * rows)
         both = lax.dot_general(
-            left, split[...], (((1,), (1,)), ((), ())), preferred_element_type=jnp.float32
-        )
-        return both[:, :n_docs] + both[:, n_docs:]
-
-    def send_part(i, carry):
-        to = (f + i) % feats
-        part[to] = score(to)
-        part_copy(to).start()
+            queries[level // halves, pl.ds(start, 2 * rows), :],
+            split[...],
+            (((1,), (1,)), ((), ())),
+            preferred_element_type=jnp.float32,
+        )
+        both = both[:, :n_docs] + both[:, n_docs:]
+        part[level * 2] = both[:rows]
+        part[level * 2 + 1] = both[rows:]
+
+    def send_parts(i, carry):
+        level = (z + i) % depth
+        score(level)
+        part_copy(level * 2 + x).start()
+        part_copy(level * 2 + 1 - x).start()
         return carry
 
-    lax.fori_loop(1, feats, send_part, 0)
-    got[f] = score(f)
+    lax.fori_loop(1, depth, send_parts, 0)
+    score(z)
+    part_copy(z * 2 + 1 - x).start()
+    got[f] = part[f]
 
     def take(i, carry):
         source = (f + i) % feats
@@ -230,6 +243,8 @@
         p, *ways = events[n]
         for way in range(3):
             when(ways[way], lambda way=way, p=p: piece_copy(p, way).wait_send())
+    for copy in detours():
+        copy.wait_send()
 
 
 def fused(feats, query_features, inverse_kernel, doc_features):
@@ -252,7 +267,7 @@
             pltpu.VMEM((feats, rows, n_docs), jnp.float32),
             pltpu.SemaphoreType.DMA((SLOTS,)),
             pltpu.SemaphoreType.DMA((PIECES,)),
-            pltpu.SemaphoreType.DMA((3, feats * PIECES)),
+            pltpu.SemaphoreType.DMA((4, feats * PIECES)),
             pltpu.SemaphoreType.DMA((feats * PIECES,)),
             pltpu.SemaphoreType.DMA((3,)),
             pltpu.SemaphoreType.DMA((feats,)),

time: 65.7 us -> 61.4 us (0.935)
  Pallas kernels: 64.1 us -> 59.9 us
    pallas_call x1, Pallas kernels: 64.1 us -> 59.9 us  [fused(): pl.pallas_call(functools.partial(kernel, feats), out_shape=jax.ShapeDtype...]
where the time goes in v1:
time: 61.4 us; the launch traced here: 61.3 us
  Pallas kernels  59.9 us (98%)
  local copies, waits for them, and re-layouts  1.42 us (2%)
    pallas_call x1, Pallas kernels, fused(): pl.pallas_call(functools.partial(kernel, feats), out_shape=jax.ShapeDtype...  59.9 us
    unnamed x1, local copies, waits for them, and re-layouts  1.42 us

profile of v1, /device:TPU:0, one launch (start us, length us, event | category | flops | bytes accessed | tf_op | source)
XLA Modules:
  0.0 61.3 jit_solution(15511161184517761749)
XLA Ops:
  0.0 59.9 %shard_map.37 = f32[96,128]{1,0:T(8,128)} custom-call(bf16[384,2048]{1,0:T(8,128)(2,1)} %q_ref.1, bf16[16384,2048]{1,0:T(8,128)(2,1)} %k_ref.1, bf16[128,2048]{1,0:T(8,128)(2,1)} %d_ref.1), custom_call_target="tpu_custom_call" | custom-call | flops 8589934592 | bytes 67108864 | tf_op jit(solution)/shard_map/pallas_call | solution.py:255
  59.9 1.4 %copy.5 = f32[96,128]{1,0:T(8,128)} copy(f32[96,128]{1,0:T(8,128)} %shard_map.37) | data formatting | bytes 98304
